TPU v7x, 512 devices: a whole 4x4x16 slice. The times are simulated.
512 devices in a mesh: blk: 16 (over x_hi, y, core), grid: 32 (over z, x_lo).
Axes of the slice: x: 4 (x_hi: 2, x_lo: 2; x = x_hi * 2 + x_lo), y: 4, z: 16, core: 2. Of those that a mesh axis runs over, the one named last changes fastest.
Arguments:
- orbitals: float32 [32, 96, 9216], P('blk', 'grid'), may hold values from -5 to 5
Outputs:
- exchange_terms: float32 [32, 96, 9216], P('blk', 'grid')
All inputs are finite; a program needn't handle non-finite values.
Results may differ from a plain program's by a relative error of at most 0.000084.
Values sent between devices are 32-bit elements; how exact they have to be, the bound alone decides.
A program may use at most 64 MiB of HBM per device.

v0:
```python
from functools import partial
import math

import jax
import jax.numpy as jnp
from jax import lax
from jax.sharding import PartitionSpec as P

NG = 96


BOX_LENGTH = 37.25
OMEGA = 0.11
contract = partial(jnp.einsum, precision=lax.Precision.HIGHEST)


def from_behind(block, axis, distance):
    devices = range(lax.axis_size(axis))
    route = [((i - distance) % len(devices), i) for i in devices]
    return lax.ppermute(block, axis, route)


def screened(squared):
    safe = jnp.where(squared > 0, squared, jnp.float32(1.0))
    value = 4.0 * math.pi / safe * (1.0 - jnp.exp(-safe / (4.0 * OMEGA * OMEGA)))
    return jnp.where(squared > 0, value, jnp.float32(math.pi / (OMEGA * OMEGA)))


def transform(real_part, imag_part, pattern, cosine, sine_table, direction):
    cos_real = contract(pattern, real_part, cosine)
    sin_real = contract(pattern, real_part, sine_table)
    cos_imag = contract(pattern, imag_part, cosine)
    sin_imag = contract(pattern, imag_part, sine_table)
    return (cos_real - direction * sin_imag, cos_imag + direction * sin_real)


def on_device(orbitals):
    orbital_count, planes, cell_count = orbitals.shape
    slab_count = lax.axis_size("grid")
    y_planes = NG // slab_count
    partner = from_behind(orbitals, "blk", 1)
    own_grid = orbitals.reshape(orbital_count, planes, NG, NG)
    partner_grid = partner.reshape(orbital_count, planes, NG, NG)
    density = (own_grid[:, None] * partner_grid[None]).reshape(
        orbital_count * orbital_count, planes, NG, NG
    )
    indices = jnp.arange(NG, dtype=jnp.int32)
    angles = (indices[:, None] * indices[None, :] % NG).astype(jnp.float32) * jnp.float32(
        2.0 * math.pi / NG
    )
    cosine = jnp.cos(angles)
    sine_table = jnp.sin(angles)
    along_z = "qxyz,zk->qxyk"
    along_y = "qxyz,yk->qxkz"
    along_x = "qxyz,xk->qkyz"
    real_part = contract(along_z, density, cosine)
    imag_part = -contract(along_z, density, sine_table)
    real_part, imag_part = transform(real_part, imag_part, along_y, cosine, sine_table, -1.0)
    pair_count = real_part.shape[0]
    stacked = jnp.stack([real_part, imag_part]).reshape(
        2, pair_count, planes, slab_count, y_planes * NG
    )
    arrived = lax.all_to_all(stacked, "grid", split_axis=3, concat_axis=2, tiled=True).reshape(
        2, pair_count, NG, y_planes, NG
    )
    real_part, imag_part = transform(arrived[0], arrived[1], along_x, cosine, sine_table, -1.0)
    wavenumber = jnp.where(indices < NG - NG // 2, indices, indices - NG).astype(
        jnp.float32
    ) * jnp.float32(2.0 * math.pi / BOX_LENGTH)
    first_row = lax.axis_index("grid") * y_planes
    local_wave = lax.dynamic_slice_in_dim(wavenumber, first_row, y_planes)
    squared = (
        wavenumber[:, None, None] ** 2
        + local_wave[None, :, None] ** 2
        + wavenumber[None, None, :] ** 2
    )
    screen = screened(squared)
    real_part = real_part * screen
    imag_part = imag_part * screen
    real_part, imag_part = transform(real_part, imag_part, along_x, cosine, sine_table, 1.0)
    stacked = jnp.stack([real_part, imag_part]).reshape(
        2, pair_count, slab_count, planes, y_planes * NG
    )
    returned_slabs = lax.all_to_all(
        stacked, "grid", split_axis=2, concat_axis=4, tiled=True
    ).reshape(2, pair_count, planes, NG, NG)
    real_part, imag_part = transform(
        returned_slabs[0], returned_slabs[1], along_y, cosine, sine_table, 1.0
    )
    inverse_norm = jnp.float32(1.0 / (NG * NG * NG))
    potential = (
        contract(along_z, real_part, cosine) - contract(along_z, imag_part, sine_table)
    ) * inverse_norm
    potential = potential.reshape(orbital_count, orbital_count, planes, cell_count)
    to_own = -contract("ijxc,jxc->ixc", potential, partner)
    to_partner = -contract("ijxc,ixc->jxc", potential, orbitals)
    returned = from_behind(to_partner, "blk", -1)
    return to_own + returned


def solution(mesh):
    in_specs = (P("blk", "grid", None),)
    out_specs = P("blk", "grid", None)
    return jax.shard_map(
        on_device, mesh=mesh, in_specs=in_specs, out_specs=out_specs, check_vma=False
    )
```

profile of v0, /device:TPU:25, one launch (start us, length us, event | category | flops | bytes accessed | tf_op | source)
XLA Modules:
  0.0 185.1 jit_solution(10606446732399162466)
XLA Ops:
  0.0 4.9 %collective-permute-start = (f32[2,3,9216]{2,0,1:T(2,128)}, f32[2,3,9216]{2,0,1:T(2,128)S(1)}, u32[]{:S(2)}, u32[]{:S(2)}) collective-permute-start(f32[2,3,9216]{2,0,1:T(2,128)} %param.1), channel_id=1, source_target_pairs={{480,0},{0,32},{32,64},{64,96},{96,128},{128,160},{160,192},{192,2... | collective-permute-start | bytes 663560 | tf_op jit(solution)/shard_map/ppermute | solution.py:20
  4.9 1.2 mul.267
  6.0 2.0 %collective-permute-done = f32[2,3,9216]{2,0,1:T(2,128)S(1)} collective-permute-done((f32[2,3,9216]{2,0,1:T(2,128)}, f32[2,3,9216]{2,0,1:T(2,128)S(1)}, u32[]{:S(2)}, u32[]{:S(2)}) %collective-permute-start) | collective-permute-done | bytes 221216 | tf_op jit(solution)/shard_map/ppermute | solution.py:20
  8.3 0.8 convolution_negate_fusion
  9.1 0.8 fusion.44
  10.0 0.9 fusion.53
  10.8 0.9 fusion.51
  11.7 0.9 fusion.14
  12.6 0.9 fusion.12
  14.6 1.3 pad_maximum_fusion
  15.9 15.4 %all-to-all-start = ((f32[2,4,3,32,288]{4,1,2,0,3:T(4,128)}), f32[2,4,3,32,288]{4,1,2,0,3:T(4,128)S(1)}, u32[]{:S(2)}, u32[]{:S(2)}) async-start(f32[2,4,3,32,288]{4,1,2,0,3:T(4,128)} %pad_maximum_fusion), calls=%async_computation | async-start | bytes 2359296 | tf_op jit(solution)/shard_map/all_to_all | solution.py:63
  31.7 57.9 %all-to-all-done = f32[2,4,3,32,288]{4,1,2,0,3:T(4,128)S(1)} async-done(((f32[2,4,3,32,288]{4,1,2,0,3:T(4,128)}), f32[2,4,3,32,288]{4,1,2,0,3:T(4,128)S(1)}, u32[]{:S(2)}, u32[]{:S(2)}) %all-to-all-start) | async-done | bytes 884768 | tf_op jit(solution)/shard_map/all_to_all | solution.py:63
  90.3 1.0 fusion.19
  91.8 1.0 fusion.15
  92.8 1.0 fusion.10
  93.8 1.0 fusion.7
  94.7 0.9 fusion.48
  95.6 0.9 fusion.56
  96.5 0.9 fusion.3
  97.4 0.9 fusion.4
  98.7 0.5 stack.21
  100.7 65.3 %all_to_all.30 = f32[2,4,32,3,288]{4,1,3,0,2:T(4,128)S(1)} all-to-all(f32[2,4,32,3,288]{4,1,3,0,2:T(4,128)S(1)} %copy.63), channel_id=1, replica_groups=mesh['blk'=16,'grid'=32] {'grid'}, dimensions={2} | all-to-all | bytes 1769472 | tf_op jit(solution)/shard_map/all_to_all | solution.py:84
  166.6 0.9 fusion.46
  167.9 0.9 fusion.58
  168.8 0.9 fusion.1
  169.7 0.9 fusion.2
  170.6 0.8 fusion.42
  171.4 0.8 fusion
  173.4 4.4 %collective-permute-start.1 = (f32[2,3,9216]{2,0,1:T(2,128)S(1)}, f32[2,3,9216]{2,0,1:T(2,128)S(1)}, u32[]{:S(2)}, u32[]{:S(2)}) collective-permute-start(f32[2,3,9216]{2,0,1:T(2,128)S(1)} %negate_bitcast_fusion), channel_id=1, source_target_pairs={{32,0},{64,32},{96,64},{128,96},{160,128},{192,160},{224,192},{256... | collective-permute-start | bytes 663560 | tf_op jit(solution)/shard_map/ppermute | solution.py:20
  177.8 1.0 fusion.22
  178.8 5.5 %collective-permute-done.1 = f32[2,3,9216]{2,0,1:T(2,128)S(1)} collective-permute-done((f32[2,3,9216]{2,0,1:T(2,128)S(1)}, f32[2,3,9216]{2,0,1:T(2,128)S(1)}, u32[]{:S(2)}, u32[]{:S(2)}) %collective-permute-start.1) | collective-permute-done | bytes 221216 | tf_op jit(solution)/shard_map/ppermute | solution.py:20
  184.2 0.8 bitcast_add_fusion
  (29 shorter events, 6.9 us)
Async XLA Ops:
  0.0 8.0 %collective-permute-start = (f32[2,3,9216]{2,0,1:T(2,128)}, f32[2,3,9216]{2,0,1:T(2,128)S(1)}, u32[]{:S(2)}, u32[]{:S(2)}) collective-permute-start(f32[2,3,9216]{2,0,1:T(2,128)} %param.1), channel_id=1, source_target_pairs={{480,0},{0,32},{32,64},{64,96},{96,128},{128,160},{160,192},{192,2... | collective-permute-start | bytes 663560 | tf_op jit(solution)/shard_map/ppermute | solution.py:20
  15.9 73.7 %all-to-all-start = ((f32[2,4,3,32,288]{4,1,2,0,3:T(4,128)}), f32[2,4,3,32,288]{4,1,2,0,3:T(4,128)S(1)}, u32[]{:S(2)}, u32[]{:S(2)}) async-start(f32[2,4,3,32,288]{4,1,2,0,3:T(4,128)} %pad_maximum_fusion), calls=%async_computation | async-start | bytes 2359296 | tf_op jit(solution)/shard_map/all_to_all | solution.py:63
  171.4 1.4 copy-start
  173.4 10.9 %collective-permute-start.1 = (f32[2,3,9216]{2,0,1:T(2,128)S(1)}, f32[2,3,9216]{2,0,1:T(2,128)S(1)}, u32[]{:S(2)}, u32[]{:S(2)}) collective-permute-start(f32[2,3,9216]{2,0,1:T(2,128)S(1)} %negate_bitcast_fusion), channel_id=1, source_target_pairs={{32,0},{64,32},{96,64},{128,96},{160,128},{192,160},{224,192},{256... | collective-permute-start | bytes 663560 | tf_op jit(solution)/shard_map/ppermute | solution.py:20
where the time goes:
time: 186 us; the launch traced here: 185 us
  waiting for transfers between devices  65.4 us (35%)
  blocking collectives  65.3 us (35%)
  starting transfers between devices  24.7 us (13%)
  matrix products  17.6 us (9%)
  local copies, waits for them, and re-layouts  7.4 us (4%)
  other arithmetic  4.31 us (2%)
    all_to_all x1, blocking collectives, on_device(): lax.all_to_all(stacked, 'grid', split_axis=2, concat_axis=4, tiled=True)  65.3 us
    all_to_all x1, waiting for transfers between devices, on_device(): lax.all_to_all(stacked, 'grid', split_axis=3, concat_axis=2, tiled=True)  57.9 us
    all_to_all x1, starting transfers between devices, on_device(): lax.all_to_all(stacked, 'grid', split_axis=3, concat_axis=2, tiled=True)  15.4 us
    ppermute x2, starting transfers between devices, from_behind(): return lax.ppermute(block, axis, route)  9.3 us
    ppermute x2, waiting for transfers between devices, from_behind(): return lax.ppermute(block, axis, route)  7.47 us
  transfers between devices with their start and end apart: 3, of which 3 were waited for; matrix products, arithmetic and copies ran while one was open for 1% of the time, Pallas kernels for 0%

commit v1 on v0

v1 whole, which is shorter than its diff:
```python
import functools
import math

import jax
import jax.numpy as jnp
import ml_dtypes
import numpy as np
from jax import lax
from jax.experimental import pallas as pl
from jax.experimental.pallas import tpu as pltpu
from jax.sharding import PartitionSpec as P

NG = 96
LANES = 128
BOX_LENGTH = 37.25
OMEGA = 0.11
SLABS = 32
PLANES = 3
ROWS = 14
PITCH = 16
MESH = pl.DeviceIdType.MESH


def split_table(table):
    high = table.astype(ml_dtypes.bfloat16)
    low = (table - high.astype(np.float64)).astype(ml_dtypes.bfloat16)
    return np.stack([high, low])


def tables():
    index = np.arange(NG)
    angle = 2.0 * np.pi / NG * ((index[:, None] * index[None, :]) % NG)
    hartley = np.cos(angle) + np.sin(angle)
    order = (np.arange(PLANES)[:, None] + PLANES * np.arange(SLABS)[None, :]).reshape(-1)
    dealt = hartley[order]
    packed = np.zeros((2 * NG, 2 * LANES))
    for i in range(2):
        packed[i * NG : (i + 1) * NG, i * LANES : i * LANES + NG] = hartley
    to_spectrum = np.concatenate([packed.T, packed.T[:, LANES : 2 * NG]], axis=1)
    from_spectrum = np.concatenate([packed, np.zeros((2 * LANES - 2 * NG, 2 * LANES))], axis=0)
    return tuple(split_table(t) for t in (dealt, dealt.T, to_spectrum, from_spectrum))


def halves(value):
    high = value.astype(jnp.bfloat16)
    low = (value - high.astype(jnp.float32)).astype(jnp.bfloat16)
    return high, low


def dot(a, b):
    return jnp.dot(a, b, preferred_element_type=jnp.float32)


def times_table(value, table):
    high, low = halves(value)
    return dot(high, table[0]) + (dot(low, table[0]) + dot(high, table[1]))


def table_times(table, value):
    high, low = halves(value)
    return dot(table[0], high) + (dot(table[0], low) + dot(table[1], high))


def signed(index):
    return jnp.where(index < NG - NG // 2, index, index - NG).astype(jnp.float32) * jnp.float32(
        2.0 * math.pi / BOX_LENGTH
    )


def screen_tile(kx, ky, kz):
    squared = signed(kx) ** 2 + signed(ky) ** 2 + signed(kz) ** 2
    safe = jnp.where(squared > 0, squared, jnp.float32(1.0))
    value = 4.0 * math.pi / safe * (1.0 - jnp.exp(-safe / (4.0 * OMEGA * OMEGA)))
    value = jnp.where(squared > 0, value, jnp.float32(math.pi / (OMEGA * OMEGA)))
    return value * jnp.float32(1.0 / (NG * NG * NG))


def kernel(
    own, dealt, dealt_t, to_spectrum, from_spectrum, out,
    partner, sent, arrived, screened, returned, screen, terms, terms_in,
    swap_send, swap_recv, send_sem, recv_sem, local_sem,
):
    me = lax.axis_index("grid")
    block = lax.axis_index("blk")
    blocks = lax.axis_size("blk")
    after = lax.rem(block + 1, blocks)
    before = lax.rem(block + blocks - 1, blocks)

    barrier = pltpu.get_barrier_semaphore()

    def greet(k, carry):
        peer = lax.rem(me + k, SLABS)
        pl.semaphore_signal(barrier, inc=1, device_id={"grid": peer}, device_id_type=MESH)
        return carry

    pl.semaphore_signal(barrier, inc=1, device_id={"blk": before}, device_id_type=MESH)
    pl.semaphore_signal(barrier, inc=1, device_id={"blk": after}, device_id_type=MESH)
    lax.fori_loop(1, SLABS, greet, 0)

    shape = (NG, LANES)
    kx = lax.broadcasted_iota(jnp.int32, shape, 0)
    lane = lax.broadcasted_iota(jnp.int32, shape, 1)
    low_half = lane < LANES // 2
    first = PLANES * me
    for r in range(PLANES):
        screen[:, r * LANES : (r + 1) * LANES] = screen_tile(
            kx, jnp.full(shape, first + r, jnp.int32), jnp.where(lane < NG, lane, lane - NG)
        )
    kz = jnp.where(low_half, lane, lane - LANES // 2) + (LANES - NG)
    screen[:, 3 * LANES : 4 * LANES] = screen_tile(kx, jnp.where(low_half, first, first + 1), kz)
    screen[:, 4 * LANES : 5 * LANES] = screen_tile(kx, jnp.full(shape, first + 2, jnp.int32), kz)

    pl.semaphore_wait(barrier, SLABS + 1)

    def swap(source, target, slot, whom):
        return pltpu.make_async_remote_copy(
            src_ref=source, dst_ref=target, send_sem=swap_send.at[slot], recv_sem=swap_recv.at[slot],
            device_id={"blk": whom}, device_id_type=MESH,
        )

    orbital_swaps = [swap(own.at[j], partner.at[j], j, after) for j in range(2)]
    for copy in orbital_swaps:
        copy.start()

    def message(source, target, slot, k, origin, peer):
        return pltpu.make_async_remote_copy(
            src_ref=source.at[peer, pl.ds(0, ROWS)],
            dst_ref=target.at[origin, pl.ds(0, ROWS)],
            send_sem=send_sem.at[slot, k],
            recv_sem=recv_sem.at[slot, origin],
            device_id={"grid": peer},
            device_id_type=MESH,
        )

    def stay(source, target, slot):
        return pltpu.make_async_copy(source.at[me], target.at[me], local_sem.at[slot])

    def scatter(source, target, slot):
        def one(k, carry):
            message(source, target, slot, k, me, lax.rem(me + k, SLABS)).start()
            return carry

        lax.fori_loop(1, SLABS, one, 0)
        stay(source, target, slot).start()

    def gather(source, target, slot):
        def one(k, carry):
            peer = lax.rem(me + k, SLABS)
            message(source, target, slot, k, peer, peer).wait_recv()
            return carry

        lax.fori_loop(1, SLABS, one, 0)
        stay(source, target, slot).wait()

    def drain(source, target, slot):
        def one(k, carry):
            message(source, target, slot, k, me, lax.rem(me + k, SLABS)).wait_send()
            return carry

        lax.fori_loop(1, SLABS, one, 0)

    def put(ref, row, value):
        ref.reshape(SLABS * PITCH, LANES)[pl.ds(row, SLABS, stride=PITCH), :] = value

    def get(ref, row):
        return ref.reshape(SLABS * PITCH, LANES)[pl.ds(row, SLABS, stride=PITCH), :]

    in_low = lax.broadcasted_iota(jnp.int32, (SLABS, LANES), 1) < LANES // 2

    def turned(value):
        return pltpu.roll(value, LANES // 2, 1)

    for j in range(2):
        orbital_swaps[j].wait_recv()
        other = partner[j]
        density = jnp.concatenate([own[0] * other, own[1] * other], axis=1)
        along_z = times_table(density, to_spectrum)
        third = []
        for x in range(PLANES):
            spectrum = table_times(dealt, along_z[x * NG : (x + 1) * NG])
            rest = []
            for r in range(PLANES):
                rows = spectrum[r * SLABS : (r + 1) * SLABS]
                put(sent.at[j], x * 4 + r, rows[:, :LANES])
                rest.append(rows[:, LANES:])
            put(sent.at[j], x * 4 + 3, jnp.where(in_low, rest[0], rest[1]))
            third.append(rest[2])
        put(sent.at[j], 12, jnp.where(in_low, third[0], third[1]))
        put(sent.at[j], 13, third[2])
        scatter(sent.at[j], arrived.at[j], j)

    for j in range(2):
        gather(sent.at[j], arrived.at[j], j)
        columns = []
        for r in range(4):
            columns.append(jnp.concatenate([get(arrived.at[j], x * 4 + r) for x in range(PLANES)], axis=0))
        pair = get(arrived.at[j], 12)
        columns.append(jnp.concatenate([pair, turned(pair), get(arrived.at[j], 13)], axis=0))
        spectrum = table_times(dealt_t, jnp.concatenate(columns, axis=1))
        back = table_times(dealt, spectrum * screen[...])
        for x in range(PLANES):
            rows = back[x * SLABS : (x + 1) * SLABS]
            for r in range(4):
                put(screened.at[j], x * 4 + r, rows[:, r * LANES : (r + 1) * LANES])
        last = back[:, 4 * LANES :]
        put(screened.at[j], 12, jnp.where(in_low, last[:SLABS], turned(last[SLABS : 2 * SLABS])))
        put(screened.at[j], 13, last[2 * SLABS :])
        scatter(screened.at[j], returned.at[j], 2 + j)

    term_swaps = [swap(terms.at[j], terms_in.at[j], 2 + j, before) for j in range(2)]
    for j in range(2):
        gather(screened.at[j], returned.at[j], 2 + j)
        pair = get(returned.at[j], 12)
        third = [pair, turned(pair), get(returned.at[j], 13)]
        planes = []
        for x in range(PLANES):
            main = jnp.concatenate([get(returned.at[j], x * 4 + r) for r in range(PLANES)], axis=0)
            both = get(returned.at[j], x * 4 + 3)
            rest = jnp.concatenate([both, turned(both), third[x]], axis=0)
            planes.append(table_times(dealt_t, jnp.concatenate([main, rest], axis=1)))
        potential = times_table(jnp.concatenate(planes, axis=0), from_spectrum)
        first_own, second_own = potential[:, :LANES], potential[:, LANES:]
        terms[j] = -(first_own * own[0] + second_own * own[1])
        term_swaps[j].start()
        other = partner[j]
        if j == 0:
            out[0] = -(first_own * other)
            out[1] = -(second_own * other)
        else:
            out[0] = out[0] - first_own * other
            out[1] = out[1] - second_own * other
    for j in range(2):
        term_swaps[j].wait_recv()
        out[j] = out[j] + terms_in[j]

    for copy in orbital_swaps + term_swaps:
        copy.wait_send()
    for j in range(2):
        drain(sent.at[j], arrived.at[j], j)
        drain(screened.at[j], returned.at[j], 2 + j)


def on_device(orbitals):
    count, planes, cells = orbitals.shape
    own = orbitals.reshape(count, planes * NG, NG)
    own = jnp.pad(own, ((0, 0), (0, 0), (0, LANES - NG)))
    vmem = pl.BlockSpec(memory_space=pltpu.VMEM)
    grid_rows = planes * NG
    messages = pltpu.VMEM((2, SLABS, PITCH, LANES), jnp.float32)
    pair = pltpu.VMEM((2, grid_rows, LANES), jnp.float32)
    terms = pl.pallas_call(
        kernel,
        out_shape=jax.ShapeDtypeStruct((count, grid_rows, LANES), jnp.float32),
        in_specs=[vmem] * 5,
        out_specs=vmem,
        scratch_shapes=[
            pair, messages, messages, messages, messages,
            pltpu.VMEM((NG, 5 * LANES), jnp.float32), pair, pair,
            pltpu.SemaphoreType.DMA((4,)), pltpu.SemaphoreType.DMA((4,)),
            pltpu.SemaphoreType.DMA((4, SLABS)), pltpu.SemaphoreType.DMA((4, SLABS)),
            pltpu.SemaphoreType.DMA((4,)),
        ],
        compiler_params=pltpu.CompilerParams(
            collective_id=0, has_side_effects=True, vmem_limit_bytes=48 * 1024 * 1024
        ),
    )(own, *tables())
    return terms[:, :, :NG].reshape(count, planes, cells)


def solution(mesh):
    spec = P("blk", "grid", None)
    return jax.shard_map(on_device, mesh=mesh, in_specs=(spec,), out_specs=spec, check_vma=False)
```

time: 186 us -> 74.9 us (0.40)
  Pallas kernels: 0 us -> 71.2 us
  waiting for transfers between devices: 65.4 us -> 0 us
  blocking collectives: 65.3 us -> 0 us
  starting transfers between devices: 24.7 us -> 0 us
  matrix products: 17.6 us -> 0 us
  other arithmetic: 4.31 us -> 0 us
  local copies, waits for them, and re-layouts: 7.4 us -> 3.4 us
    pallas_call x0 -> x1, Pallas kernels: none -> 71.2 us  [on_device(): pl.pallas_call(kernel, out_shape=jax.ShapeDtypeStruct((count, grid_rows,...]
    all_to_all x1 -> x0, blocking collectives: 65.3 us -> none  [on_device(): lax.all_to_all(stacked, 'grid', split_axis=2, concat_axis=4, tiled=True)]
    all_to_all x1 -> x0, waiting for transfers between devices: 57.9 us -> none  [on_device(): lax.all_to_all(stacked, 'grid', split_axis=3, concat_axis=2, tiled=True)]
    dot_general x20 -> x0, matrix products: 17.6 us -> none  [the longest x4 3.61 us: transform(): sin_imag = contract(pattern, imag_part, sine_table)]
    all_to_all x1 -> x0, starting transfers between devices: 15.4 us -> none  [on_device(): lax.all_to_all(stacked, 'grid', split_axis=3, concat_axis=2, tiled=True)]
    ppermute x2 -> x0, starting transfers between devices: 9.3 us -> none  [from_behind(): return lax.ppermute(block, axis, route)]
    ppermute x2 -> x0, waiting for transfers between devices: 7.47 us -> none  [from_behind(): return lax.ppermute(block, axis, route)]
    another operation x7 -> x0, local copies, waits for them, and re-layouts: 2.43 us -> none  [on_device(): jnp.stack([real_part, imag_part])]
  transfers between devices with their start and end apart: 3 -> 0, of which waited for: 3 -> 0; matrix products, arithmetic and copies ran while one was open for 1% -> 0% of each run, Pallas kernels for 0% -> 0%
where the time goes in v1:
time: 74.9 us; the launch traced here: 74.6 us
  Pallas kernels  71.2 us (95%)
  local copies, waits for them, and re-layouts  3.4 us (5%)
    pallas_call x1, Pallas kernels, on_device(): pl.pallas_call(kernel, out_shape=jax.ShapeDtypeStruct((count, grid_rows,...  71.2 us
    unnamed x9, local copies, waits for them, and re-layouts  2.04 us

profile of v1, /device:TPU:25, one launch (start us, length us, event | category | flops | bytes accessed | tf_op | source)
XLA Modules:
  0.0 74.6 jit_solution(9776573756184178189)
XLA Ops:
  0.0 1.1 %copy.8 = f32[2,3,9216]{2,1,0:T(4,128)S(1)} copy(f32[2,3,9216]{2,0,1:T(2,128)} %param.5) | data formatting | bytes 442368 | tf_op args[0]
  1.1 0.0 copy-start.3
  1.1 0.2 reshape.6
  1.3 0.0 copy-start
  1.3 0.0 copy-start.1
  1.3 0.0 copy-start.2
  1.3 0.5 copy-done.3
  1.9 0.4 copy-done
  2.2 0.1 copy-done.1
  2.3 0.0 copy-done.2
  2.3 71.2 %shard_map.55 = f32[2,288,128]{2,1,0:T(8,128)S(1)} custom-call(f32[2,288,128]{2,1,0:T(8,128)S(1)} %pad.4.own, bf16[2,96,96]{2,1,0:T(8,128)(2,1)S(1)} %copy-done.3, bf16[2,96,96]{2,1,0:T(8,128)(2,1)S(1)} %copy-done.2, bf16[2,256,256]{2,1,0:T(8,128)(2,1)S(1)} %copy-done.1, bf16[2,256,256]{2,1,0:T(8,128)(2,1)S(1)} %copy-done), custom_call_target="tpu_custom_call" | custom-call | tf_op jit(solution)/shard_map/pallas_call | solution.py:251
  73.5 0.3 reshape.7
  73.8 0.9 %copy.9 = f32[2,3,9216]{2,0,1:T(2,128)} copy(f32[2,3,9216]{2,1,0:T(4,128)S(1)} %reshape.7) | data formatting | bytes 442368 | tf_op jit(solution)/shard_map/reshape | solution.py:267
  (1 shorter events, 0.0 us)
Async XLA Ops:
  1.1 0.8 %copy-start.3 = (bf16[2,96,96]{2,1,0:T(8,128)(2,1)S(1)}, bf16[2,96,96]{2,1,0:T(8,128)(2,1)}, u32[]{:S(2)}) copy-start(bf16[2,96,96]{2,1,0:T(8,128)(2,1)} %constant.11.clone.dealt) | copy-start | bytes 110596
  1.3 1.0 %copy-start = (bf16[2,256,256]{2,1,0:T(8,128)(2,1)S(1)}, bf16[2,256,256]{2,1,0:T(8,128)(2,1)}, u32[]{:S(2)}) copy-start(bf16[2,256,256]{2,1,0:T(8,128)(2,1)} %constant.14.clone.from_spectrum) | copy-start | bytes 786436
  1.3 1.0 %copy-start.1 = (bf16[2,256,256]{2,1,0:T(8,128)(2,1)S(1)}, bf16[2,256,256]{2,1,0:T(8,128)(2,1)}, u32[]{:S(2)}) copy-start(bf16[2,256,256]{2,1,0:T(8,128)(2,1)} %constant.13.clone.to_spectrum) | copy-start | bytes 786436
  1.3 1.0 %copy-start.2 = (bf16[2,96,96]{2,1,0:T(8,128)(2,1)S(1)}, bf16[2,96,96]{2,1,0:T(8,128)(2,1)}, u32[]{:S(2)}) copy-start(bf16[2,96,96]{2,1,0:T(8,128)(2,1)} %constant.12.clone.dealt_t) | copy-start | bytes 110596

commit v2 on v1

v2 whole, which is shorter than its diff:
```python
import math

import jax
import jax.numpy as jnp
import numpy as np
from jax import lax
from jax.experimental import pallas as pl
from jax.experimental.pallas import tpu as pltpu
from jax.sharding import PartitionSpec as P

NG = 96
LANES = 128
HALF = LANES // 2
BOX_LENGTH = 37.25
OMEGA = 0.11
SLABS = 32
PLANES = 3
TILES = NG * NG // LANES
TURN = 4
TURNS = NG // TURN
MAIN = 4 * PLANES
MAIN_PITCH = 16
REST = PLANES
REST_PITCH = 8
MESH = pl.DeviceIdType.MESH
FAR_FIRST = sorted(range(1, SLABS), key=lambda k: abs(k - SLABS // 2))


def tables():
    index = np.arange(NG)
    angle = 2.0 * np.pi / NG * ((index[:, None] * index[None, :]) % NG)
    hartley = np.cos(angle) + np.sin(angle)
    by_slab = (np.arange(PLANES)[:, None] + PLANES * np.arange(SLABS)[None, :]).reshape(-1)
    by_turn = (np.arange(TURN)[:, None] + TURN * np.arange(TURNS)[None, :]).reshape(-1)
    dealt = hartley[by_slab][:, by_turn]
    packed = np.zeros((2 * NG, 2 * LANES))
    for i in range(2):
        packed[i * NG : (i + 1) * NG, i * LANES : i * LANES + NG] = hartley
    to_spectrum = np.concatenate([packed.T, packed.T[:, LANES : 2 * NG]], axis=1)
    from_spectrum = np.concatenate([packed, np.zeros((2 * LANES - 2 * NG, 2 * LANES))], axis=0)
    return tuple(t.astype(np.float32) for t in (dealt, dealt.T, to_spectrum, from_spectrum))


def halves(value):
    high = value.astype(jnp.bfloat16)
    low = (value - high.astype(jnp.float32)).astype(jnp.bfloat16)
    return high, low


def dot(a, b):
    return jnp.dot(a, b, preferred_element_type=jnp.float32)


def times_table(value, table):
    high, low = halves(value)
    return dot(high, table[0]) + (dot(low, table[0]) + dot(high, table[1]))


def table_times(table, value):
    high, low = halves(value)
    return dot(table[0], high) + (dot(table[0], low) + dot(table[1], high))


def signed(index):
    return jnp.where(index < NG - NG // 2, index, index - NG).astype(jnp.float32) * jnp.float32(
        2.0 * math.pi / BOX_LENGTH
    )


def screen_tile(kx, ky, kz):
    squared = signed(kx) ** 2 + signed(ky) ** 2 + signed(kz) ** 2
    safe = jnp.where(squared > 0, squared, jnp.float32(1.0))
    value = 4.0 * math.pi / safe * (1.0 - jnp.exp(-safe / (4.0 * OMEGA * OMEGA)))
    value = jnp.where(squared > 0, value, jnp.float32(math.pi / (OMEGA * OMEGA)))
    return value * jnp.float32(1.0 / (NG * NG * NG))


def turned(value, by=HALF):
    return pltpu.roll(value, by, 1)


def unpacked(flat, x):
    a, b, c = (flat[pl.ds(x * TILES + k, TURNS, stride=3), :] for k in range(3))
    lane = lax.broadcasted_iota(jnp.int32, a.shape, 1)
    second = jnp.where(lane < 32, turned(a, 32), turned(b, 32))
    third = jnp.where(lane < HALF, turned(b), turned(c))
    return jnp.concatenate([a, second, third, turned(c, 96)], axis=0)


def packed_rows(plane):
    first, second, third, fourth = (plane[k * TURNS : (k + 1) * TURNS] for k in range(TURN))
    lane = lax.broadcasted_iota(jnp.int32, first.shape, 1)
    second, third = turned(second, 96), turned(third)
    return (
        jnp.where(lane < NG, first, second),
        jnp.where(lane < HALF, second, third),
        jnp.where(lane < 32, third, turned(fourth, 32)),
    )


def put(ref, row, value):
    pitch = ref.shape[1]
    ref.reshape(SLABS * pitch, LANES)[pl.ds(row, SLABS, stride=pitch), :] = value


def get(ref, row):
    pitch = ref.shape[1]
    return ref.reshape(SLABS * pitch, LANES)[pl.ds(row, SLABS, stride=pitch), :]


def kernel(
    orbitals, dealt_in, dealt_t_in, to_spectrum_in, from_spectrum_in, out,
    raw, dealt_raw, dealt_t_raw, to_spectrum_raw, from_spectrum_raw,
    dealt, dealt_t, to_spectrum, from_spectrum,
    own_flat, own, partner_flat, partner, to_own,
    sent, arrived, screened, returned, sent_rest, arrived_rest, screened_rest, returned_rest,
    screen, terms, terms_in,
    load_sem, swap_send, swap_recv, send_sem, recv_sem, local_sem,
):
    me = lax.axis_index("grid")
    block = lax.axis_index("blk")
    blocks = lax.axis_size("blk")
    after = lax.rem(block + 1, blocks)
    before = lax.rem(block + blocks - 1, blocks)
    peers = {k: lax.rem(me + k, SLABS) for k in FAR_FIRST}

    barrier = pltpu.get_barrier_semaphore()
    for k in FAR_FIRST:
        pl.semaphore_signal(barrier, inc=1, device_id={"grid": peers[k]}, device_id_type=MESH)
    for neighbour in (before, after):
        pl.semaphore_signal(barrier, inc=1, device_id={"blk": neighbour}, device_id_type=MESH)

    loads = [
        pltpu.make_async_copy(source, target, load_sem.at[k])
        for k, (source, target) in enumerate(
            [
                (orbitals, raw),
                (to_spectrum_in, to_spectrum_raw),
                (dealt_in, dealt_raw),
                (dealt_t_in, dealt_t_raw),
                (from_spectrum_in, from_spectrum_raw),
            ]
        )
    ]
    for load in loads:
        load.start()

    shape = (NG, LANES)
    row = lax.broadcasted_iota(jnp.int32, shape, 0)
    turn = (row >= TURNS).astype(jnp.int32) + (row >= 2 * TURNS) + (row >= 3 * TURNS)
    kx = TURN * (row - TURNS * turn) + turn
    lane = lax.broadcasted_iota(jnp.int32, shape, 1)
    low_half = lane < HALF
    first = PLANES * me
    for r in range(PLANES):
        screen[:, r * LANES : (r + 1) * LANES] = screen_tile(
            kx, jnp.full(shape, first + r, jnp.int32), jnp.where(lane < NG, lane, lane - NG)
        )
    kz = jnp.where(low_half, lane, lane - HALF) + (LANES - NG)
    screen[:, 3 * LANES : 4 * LANES] = screen_tile(kx, jnp.where(low_half, first, first + 1), kz)
    screen[:, 4 * LANES : 5 * LANES] = screen_tile(kx, jnp.full(shape, first + 2, jnp.int32), kz)

    loads[0].wait()
    for i in range(2):
        own_flat[i] = raw[pl.ds(i, PLANES * TILES, stride=2), :]
        for x in range(PLANES):
            own[i, x * NG : (x + 1) * NG] = unpacked(own_flat.at[i], x)
    for load in loads[1:]:
        load.wait()
    for source, target in (
        (to_spectrum_raw, to_spectrum),
        (dealt_raw, dealt),
        (dealt_t_raw, dealt_t),
        (from_spectrum_raw, from_spectrum),
    ):
        target[0], target[1] = halves(source[...])

    pl.semaphore_wait(barrier, SLABS + 1)

    def swap(source, target, slot, whom):
        return pltpu.make_async_remote_copy(
            src_ref=source, dst_ref=target, send_sem=swap_send.at[slot], recv_sem=swap_recv.at[slot],
            device_id={"blk": whom}, device_id_type=MESH,
        )

    orbital_swaps = [swap(own_flat.at[j], partner_flat.at[j], j, after) for j in range(2)]
    for copy in orbital_swaps:
        copy.start()

    def message(source, target, rows, slot, k, origin, peer):
        return pltpu.make_async_remote_copy(
            src_ref=source.at[peer, pl.ds(0, rows)],
            dst_ref=target.at[origin, pl.ds(0, rows)],
            send_sem=send_sem.at[slot, k],
            recv_sem=recv_sem.at[slot, origin],
            device_id={"grid": peer},
            device_id_type=MESH,
        )

    def stay(source, target, rows, slot):
        return pltpu.make_async_copy(source.at[me], target.at[me], local_sem.at[slot])

    def scatter(*job):
        source, target, rows, slot = job
        for k in FAR_FIRST:
            message(*job, k, me, peers[k]).start()
        stay(*job).start()

    def gather(*job):
        for k in FAR_FIRST:
            message(*job, k, peers[k], peers[k]).wait_recv()
        stay(*job).wait()

    def drain(*job):
        for k in FAR_FIRST:
            message(*job, k, me, peers[k]).wait_send()

    out_jobs = [(sent.at[j], arrived.at[j], MAIN, j) for j in range(2)]
    out_rest = (sent_rest, arrived_rest, REST, 2)
    back_jobs = [(screened.at[j], returned.at[j], MAIN, 3 + j) for j in range(2)]
    back_rest = (screened_rest, returned_rest, REST, 5)

    in_low = lax.broadcasted_iota(jnp.int32, (SLABS, LANES), 1) < HALF

    thirds = []
    for j in range(2):
        orbital_swaps[j].wait_recv()
        for x in range(PLANES):
            plane = pl.ds(x * NG, NG)
            other = unpacked(partner_flat.at[j], x)
            partner[j, plane] = other
            density = jnp.concatenate([own[0, plane] * other, own[1, plane] * other], axis=1)
            spectrum = table_times(dealt, times_table(density, to_spectrum))
            rest = []
            for r in range(PLANES):
                rows = spectrum[r * SLABS : (r + 1) * SLABS]
                put(sent.at[j], x * 4 + r, rows[:, :LANES])
                rest.append(rows[:, LANES:])
            put(sent.at[j], x * 4 + 3, jnp.where(in_low, rest[0], rest[1]))
            if j == 0:
                thirds.append(rest[2])
            else:
                put(sent_rest, x, jnp.where(in_low, thirds[x], rest[2]))
        if j == 1:
            scatter(*out_rest)
        scatter(*out_jobs[j])

    def along_x(source, target, width, start):
        columns = []
        for c in range(width):
            columns.append(jnp.concatenate([get(source, x * width + c) for x in range(PLANES)], axis=0))
        spectrum = table_times(dealt_t, jnp.concatenate(columns, axis=1))
        back = table_times(dealt, spectrum * screen[:, start * LANES : (start + width) * LANES])
        for x in range(PLANES):
            rows = back[x * SLABS : (x + 1) * SLABS]
            for c in range(width):
                put(target, x * width + c, rows[:, c * LANES : (c + 1) * LANES])

    gather(*out_jobs[0])
    along_x(arrived.at[0], screened.at[0], 4, 0)
    scatter(*back_jobs[0])
    gather(*out_rest)
    along_x(arrived_rest, screened_rest, 1, 4)
    scatter(*back_rest)
    gather(*out_jobs[1])
    along_x(arrived.at[1], screened.at[1], 4, 0)
    scatter(*back_jobs[1])

    term_swaps = [swap(terms.at[j], terms_in.at[j], 2 + j, before) for j in range(2)]
    gather(*back_rest)
    for j in range(2):
        gather(*back_jobs[j])
        for x in range(PLANES):
            plane = pl.ds(x * NG, NG)
            main = jnp.concatenate([get(returned.at[j], x * 4 + r) for r in range(PLANES)], axis=0)
            both = get(returned.at[j], x * 4 + 3)
            last = get(returned_rest, x)
            if j == 1:
                last = turned(last)
            rest = jnp.concatenate([both, turned(both), last], axis=0)
            potential = times_table(
                table_times(dealt_t, jnp.concatenate([main, rest], axis=1)), from_spectrum
            )
            parts = [potential[:, :LANES], potential[:, LANES:]]
            term = -(parts[0] * own[0, plane] + parts[1] * own[1, plane])
            for k, value in enumerate(packed_rows(term)):
                terms[j, pl.ds(x * TILES + k, TURNS, stride=3), :] = value
            for i in range(2):
                mine = parts[i] * partner[j, plane]
                if j == 0:
                    to_own[i, plane] = -mine
                else:
                    to_own[i, plane] = to_own[i, plane] - mine
        term_swaps[j].start()
    for i in range(2):
        term_swaps[i].wait_recv()
        for x in range(PLANES):
            for k, value in enumerate(packed_rows(to_own[i, pl.ds(x * NG, NG)])):
                theirs = terms_in[i, pl.ds(x * TILES + k, TURNS, stride=3), :]
                out[pl.ds((x * TILES + k) * 2 + i, TURNS, stride=6), :] = value + theirs

    for copy in orbital_swaps + term_swaps:
        copy.wait_send()
    for job in out_jobs + [out_rest] + back_jobs + [back_rest]:
        drain(*job)


def on_device(orbitals):
    count, planes, cells = orbitals.shape
    flat = orbitals.reshape(count, planes, TILES, LANES).transpose(1, 2, 0, 3)
    flat = flat.reshape(planes * TILES * count, LANES)
    vmem = pl.BlockSpec(memory_space=pltpu.VMEM)
    hbm = pl.BlockSpec(memory_space=pltpu.HBM)
    constants = tables()

    def scratch(*shape):
        return pltpu.VMEM(shape, jnp.float32)

    main, rest = scratch(2, SLABS, MAIN_PITCH, LANES), scratch(SLABS, REST_PITCH, LANES)
    as_it_lies, padded = scratch(2, planes * TILES, LANES), scratch(2, planes * NG, LANES)
    terms = pl.pallas_call(
        kernel,
        out_shape=jax.ShapeDtypeStruct(flat.shape, jnp.float32),
        in_specs=[hbm] * 5,
        out_specs=vmem,
        scratch_shapes=[
            scratch(*flat.shape), *(scratch(*t.shape) for t in constants),
            *(pltpu.VMEM((2, *t.shape), jnp.bfloat16) for t in constants),
            as_it_lies, padded, as_it_lies, padded, padded,
            main, main, main, main, rest, rest, rest, rest,
            scratch(NG, 5 * LANES), as_it_lies, as_it_lies,
            pltpu.SemaphoreType.DMA((5,)),
            pltpu.SemaphoreType.DMA((4,)), pltpu.SemaphoreType.DMA((4,)),
            pltpu.SemaphoreType.DMA((6, SLABS)), pltpu.SemaphoreType.DMA((6, SLABS)),
            pltpu.SemaphoreType.DMA((6,)),
        ],
        compiler_params=pltpu.CompilerParams(
            collective_id=0, has_side_effects=True, vmem_limit_bytes=60 * 1024 * 1024
        ),
    )(flat, *constants)
    terms = terms.reshape(planes, TILES, count, LANES).transpose(2, 0, 1, 3)
    return terms.reshape(count, planes, cells)


def solution(mesh):
    spec = P("blk", "grid", None)
    return jax.shard_map(on_device, mesh=mesh, in_specs=(spec,), out_specs=spec, check_vma=False)
```

time: 74.9 us -> 70.5 us (0.941)
  Pallas kernels: 71.2 us -> 68.6 us
  local copies, waits for them, and re-layouts: 3.4 us -> 1.64 us
    pallas_call x1, Pallas kernels: 71.2 us -> 68.6 us  [on_device(): pl.pallas_call(kernel, out_shape=jax.ShapeDtypeStruct(flat.shape, jnp.flo...]
    reshape x3 -> x0, local copies, waits for them, and re-layouts: 1.34 us -> none  [the longest x2 1.15 us: on_device(): return terms[:, :, :NG].reshape(count, planes, cells)]
    unnamed x9 -> x1, local copies, waits for them, and re-layouts: 2.04 us -> 1.64 us
where the time goes in v2:
time: 70.5 us; the launch traced here: 70.3 us
  Pallas kernels  68.6 us (97%)
  local copies, waits for them, and re-layouts  1.64 us (2%)
    pallas_call x1, Pallas kernels, on_device(): pl.pallas_call(kernel, out_shape=jax.ShapeDtypeStruct(flat.shape, jnp.flo...  68.6 us
    unnamed x1, local copies, waits for them, and re-layouts  1.64 us

profile of v2, /device:TPU:25, one launch (start us, length us, event | category | flops | bytes accessed | tf_op | source)
XLA Modules:
  0.0 70.3 jit_solution(6491714819556007288)
XLA Ops:
  0.0 68.6 %shard_map.55 = f32[432,128]{1,0:T(8,128)} custom-call(f32[432,128]{1,0:T(8,128)} %bitcast.11, f32[96,96]{1,0:T(8,128)} %constant.8.clone.dealt_in, f32[96,96]{1,0:T(8,128)} %constant.9.clone.dealt_t_in, f32[256,256]{1,0:T(8,128)} %constant.10.clone.to_spectrum_in, f32[256,256]{1,0:T(8,128)} %constant.11.clone.from_spectrum_in), custom_call_target="tpu_custom_call" | custom-call | tf_op jit(solution)/shard_map/pallas_call | solution.py:321
  68.7 1.6 %copy.9 = f32[2,3,9216]{2,0,1:T(2,128)} copy(f32[2,3,9216]{2,0,1:T(2,128)} %bitcast.10) | data formatting | bytes 442368

commit v3 on v2

--- a/solution.py
+++ b/solution.py
@@ -19,8 +19,8 @@
 TURN = 4
 TURNS = NG // TURN
 MAIN = 4 * PLANES
+REST = PLANES
 MAIN_PITCH = 16
-REST = PLANES
 REST_PITCH = 8
 MESH = pl.DeviceIdType.MESH
 FAR_FIRST = sorted(range(1, SLABS), key=lambda k: abs(k - SLABS // 2))
@@ -113,9 +113,9 @@
     raw, dealt_raw, dealt_t_raw, to_spectrum_raw, from_spectrum_raw,
     dealt, dealt_t, to_spectrum, from_spectrum,
     own_flat, own, partner_flat, partner, to_own,
-    sent, arrived, screened, returned, sent_rest, arrived_rest, screened_rest, returned_rest,
+    sent, arrived, screened, returned, screened_rest, returned_rest,
     screen, terms, terms_in,
-    load_sem, swap_send, swap_recv, send_sem, recv_sem, local_sem,
+    load_sem, swap_send, swap_recv, send_sem, recv_sem, local_sem, turn_sem,
 ):
     me = lax.axis_index("grid")
     block = lax.axis_index("blk")
@@ -215,10 +215,9 @@
         for k in FAR_FIRST:
             message(*job, k, me, peers[k]).wait_send()
 
-    out_jobs = [(sent.at[j], arrived.at[j], MAIN, j) for j in range(2)]
-    out_rest = (sent_rest, arrived_rest, REST, 2)
-    back_jobs = [(screened.at[j], returned.at[j], MAIN, 3 + j) for j in range(2)]
-    back_rest = (screened_rest, returned_rest, REST, 5)
+    out_jobs = [(sent.at[j], arrived.at[j], MAIN + REST * j, j) for j in range(2)]
+    back_jobs = [(screened.at[j], returned.at[j], MAIN, 2 + j) for j in range(2)]
+    back_rest = (screened_rest, returned_rest, REST, 4)
 
     in_low = lax.broadcasted_iota(jnp.int32, (SLABS, LANES), 1) < HALF
 
@@ -240,31 +239,44 @@
             if j == 0:
                 thirds.append(rest[2])
             else:
-                put(sent_rest, x, jnp.where(in_low, thirds[x], rest[2]))
-        if j == 1:
-            scatter(*out_rest)
+                put(sent.at[j], MAIN + x, jnp.where(in_low, thirds[x], rest[2]))
         scatter(*out_jobs[j])
 
-    def along_x(source, target, width, start):
+    def along_x(source, start, width, tile):
         columns = []
         for c in range(width):
-            columns.append(jnp.concatenate([get(source, x * width + c) for x in range(PLANES)], axis=0))
+            rows = [get(source, start + x * width + c) for x in range(PLANES)]
+            columns.append(jnp.concatenate(rows, axis=0))
         spectrum = table_times(dealt_t, jnp.concatenate(columns, axis=1))
-        back = table_times(dealt, spectrum * screen[:, start * LANES : (start + width) * LANES])
+        return table_times(dealt, spectrum * screen[:, tile * LANES : (tile + width) * LANES])
+
+    def deal(target, back, width):
         for x in range(PLANES):
             rows = back[x * SLABS : (x + 1) * SLABS]
             for c in range(width):
                 put(target, x * width + c, rows[:, c * LANES : (c + 1) * LANES])
 
     gather(*out_jobs[0])
-    along_x(arrived.at[0], screened.at[0], 4, 0)
+    deal(screened.at[0], along_x(arrived.at[0], 0, 4, 0), 4)
     scatter(*back_jobs[0])
-    gather(*out_rest)
-    along_x(arrived_rest, screened_rest, 1, 4)
+    gather(*out_jobs[1])
+    deal(screened_rest, along_x(arrived.at[1], MAIN, 1, 4), 1)
     scatter(*back_rest)
-    gather(*out_jobs[1])
-    along_x(arrived.at[1], screened.at[1], 4, 0)
+    deal(screened.at[1], along_x(arrived.at[1], 0, 4, 0), 4)
+    odd = lax.rem(block, 2) == 1
+
+    @pl.when(odd)
+    def _():
+        pl.semaphore_wait(turn_sem, 1)
+
     scatter(*back_jobs[1])
+
+    @pl.when(jnp.logical_not(odd))
+    def _():
+        for k in FAR_FIRST[:24]:
+            message(*back_jobs[1], k, me, peers[k]).wait_send()
+        pl.semaphore_signal(turn_sem, inc=1, device_id={"blk": after}, device_id_type=MESH)
+
 
     term_swaps = [swap(terms.at[j], terms_in.at[j], 2 + j, before) for j in range(2)]
     gather(*back_rest)
@@ -301,8 +313,15 @@
 
     for copy in orbital_swaps + term_swaps:
         copy.wait_send()
-    for job in out_jobs + [out_rest] + back_jobs + [back_rest]:
+    for job in [*out_jobs, back_jobs[0], back_rest]:
         drain(*job)
+    for k in FAR_FIRST[24:]:
+        message(*back_jobs[1], k, me, peers[k]).wait_send()
+
+    @pl.when(odd)
+    def _():
+        for k in FAR_FIRST[:24]:
+            message(*back_jobs[1], k, me, peers[k]).wait_send()
 
 
 def on_device(orbitals):
@@ -327,12 +346,12 @@
             scratch(*flat.shape), *(scratch(*t.shape) for t in constants),
             *(pltpu.VMEM((2, *t.shape), jnp.bfloat16) for t in constants),
             as_it_lies, padded, as_it_lies, padded, padded,
-            main, main, main, main, rest, rest, rest, rest,
+            main, main, main, main, rest, rest,
             scratch(NG, 5 * LANES), as_it_lies, as_it_lies,
             pltpu.SemaphoreType.DMA((5,)),
             pltpu.SemaphoreType.DMA((4,)), pltpu.SemaphoreType.DMA((4,)),
-            pltpu.SemaphoreType.DMA((6, SLABS)), pltpu.SemaphoreType.DMA((6, SLABS)),
-            pltpu.SemaphoreType.DMA((6,)),
+            pltpu.SemaphoreType.DMA((5, SLABS)), pltpu.SemaphoreType.DMA((5, SLABS)),
+            pltpu.SemaphoreType.DMA((5,)), pltpu.SemaphoreType.REGULAR,
         ],
         compiler_params=pltpu.CompilerParams(
             collective_id=0, has_side_effects=True, vmem_limit_bytes=60 * 1024 * 1024

time: 70.5 us -> 66.7 us (0.946)
  Pallas kernels: 68.6 us -> 64.4 us
    pallas_call x1, Pallas kernels: 68.6 us -> 64.4 us  [on_device(): pl.pallas_call(kernel, out_shape=jax.ShapeDtypeStruct(flat.shape, jnp.flo...]
where the time goes in v3:
time: 66.7 us; the launch traced here: 66.1 us
  Pallas kernels  64.4 us (97%)
  local copies, waits for them, and re-layouts  1.64 us (2%)
    pallas_call x1, Pallas kernels, on_device(): pl.pallas_call(kernel, out_shape=jax.ShapeDtypeStruct(flat.shape, jnp.flo...  64.4 us
    unnamed x1, local copies, waits for them, and re-layouts  1.64 us

profile of v3, /device:TPU:25, one launch (start us, length us, event | category | flops | bytes accessed | tf_op | source)
XLA Modules:
  0.0 66.1 jit_solution(4315795490171468782)
XLA Ops:
  0.0 64.4 %shard_map.55 = f32[432,128]{1,0:T(8,128)} custom-call(f32[432,128]{1,0:T(8,128)} %bitcast.11, f32[96,96]{1,0:T(8,128)} %constant.8.clone.dealt_in, f32[96,96]{1,0:T(8,128)} %constant.9.clone.dealt_t_in, f32[256,256]{1,0:T(8,128)} %constant.10.clone.to_spectrum_in, f32[256,256]{1,0:T(8,128)} %constant.11.clone.from_spectrum_in), custom_call_target="tpu_custom_call" | custom-call | tf_op jit(solution)/shard_map/pallas_call | solution.py:340
  64.4 1.6 %copy.9 = f32[2,3,9216]{2,0,1:T(2,128)} copy(f32[2,3,9216]{2,0,1:T(2,128)} %bitcast.10) | data formatting | bytes 442368

commit v4 on v3

--- a/solution.py
+++ b/solution.py
@@ -354,9 +354,9 @@
             pltpu.SemaphoreType.DMA((5,)), pltpu.SemaphoreType.REGULAR,
         ],
         compiler_params=pltpu.CompilerParams(
-            collective_id=0, has_side_effects=True, vmem_limit_bytes=60 * 1024 * 1024
+            collective_id=0, has_side_effects=True, vmem_limit_bytes=32 * 1024 * 1024
         ),
-    )(flat, *constants)
+    )(*(pltpu.with_memory_space_constraint(a, pltpu.HBM) for a in (flat, *map(jnp.asarray, constants))))
     terms = terms.reshape(planes, TILES, count, LANES).transpose(2, 0, 1, 3)
     return terms.reshape(count, planes, cells)
 

time: 66.7 us -> 65.1 us (0.976)
  local copies, waits for them, and re-layouts: 1.64 us -> 0.69 us
  Pallas kernels: 64.4 us -> 63.7 us
    unnamed x1, local copies, waits for them, and re-layouts: 1.64 us -> 0.69 us
    pallas_call x1, Pallas kernels: 64.4 us -> 63.7 us  [on_device(): pl.pallas_call(kernel, out_shape=jax.ShapeDtypeStruct(flat.shape, jnp.flo...]
where the time goes in v4:
time: 65.1 us; the launch traced here: 64.4 us
  Pallas kernels  63.7 us (98%)
  local copies, waits for them, and re-layouts  0.69 us (1%)
    pallas_call x1, Pallas kernels, on_device(): pl.pallas_call(kernel, out_shape=jax.ShapeDtypeStruct(flat.shape, jnp.flo...  63.7 us

profile of v4, /device:TPU:25, one launch (start us, length us, event | category | flops | bytes accessed | tf_op | source)
XLA Modules:
  0.0 64.4 jit_solution(11732092468524803124)
XLA Ops:
  0.0 63.7 %shard_map.55 = f32[432,128]{1,0:T(8,128)S(1)} custom-call(f32[432,128]{1,0:T(8,128)} %bitcast.11, f32[96,96]{1,0:T(8,128)} %constant.8.clone.dealt_in, f32[96,96]{1,0:T(8,128)} %constant.9.clone.dealt_t_in, f32[256,256]{1,0:T(8,128)} %constant.10.clone.to_spectrum_in, f32[256,256]{1,0:T(8,128)} %constant.11.clone.from_spectrum_in), custom_call_target="tpu_custom_call" | custom-call | tf_op jit(solution)/shard_map/pallas_call | solution.py:340
  63.7 0.7 %copy.9 = f32[2,3,9216]{2,0,1:T(2,128)} copy(f32[2,3,9216]{2,0,1:T(2,128)S(1)} %bitcast.10) | data formatting | bytes 442368

commit v5 on v4

--- a/solution.py
+++ b/solution.py
@@ -277,6 +277,10 @@
             message(*back_jobs[1], k, me, peers[k]).wait_send()
         pl.semaphore_signal(turn_sem, inc=1, device_id={"blk": after}, device_id_type=MESH)
 
+    for copy in orbital_swaps:
+        copy.wait_send()
+    for job in out_jobs:
+        drain(*job)
 
     term_swaps = [swap(terms.at[j], terms_in.at[j], 2 + j, before) for j in range(2)]
     gather(*back_rest)
@@ -304,17 +308,9 @@
                 else:
                     to_own[i, plane] = to_own[i, plane] - mine
         term_swaps[j].start()
-    for i in range(2):
-        term_swaps[i].wait_recv()
-        for x in range(PLANES):
-            for k, value in enumerate(packed_rows(to_own[i, pl.ds(x * NG, NG)])):
-                theirs = terms_in[i, pl.ds(x * TILES + k, TURNS, stride=3), :]
-                out[pl.ds((x * TILES + k) * 2 + i, TURNS, stride=6), :] = value + theirs
-
-    for copy in orbital_swaps + term_swaps:
-        copy.wait_send()
-    for job in [*out_jobs, back_jobs[0], back_rest]:
-        drain(*job)
+        if j == 0:
+            drain(*back_jobs[0])
+            drain(*back_rest)
     for k in FAR_FIRST[24:]:
         message(*back_jobs[1], k, me, peers[k]).wait_send()
 
@@ -322,6 +318,16 @@
     def _():
         for k in FAR_FIRST[:24]:
             message(*back_jobs[1], k, me, peers[k]).wait_send()
+
+    for i in range(2):
+        term_swaps[i].wait_recv()
+        for x in range(PLANES):
+            for k, value in enumerate(packed_rows(to_own[i, pl.ds(x * NG, NG)])):
+                theirs = terms_in[i, pl.ds(x * TILES + k, TURNS, stride=3), :]
+                out[pl.ds((x * TILES + k) * 2 + i, TURNS, stride=6), :] = value + theirs
+
+    for copy in term_swaps:
+        copy.wait_send()
 
 
 def on_device(orbitals):

time: 65.1 us -> 64.8 us (level)
  no operation moved by 1% of the time
where the time goes in v5:
time: 64.8 us; the launch traced here: 64.2 us
  Pallas kernels  63.5 us (98%)
  local copies, waits for them, and re-layouts  0.69 us (1%)
    pallas_call x1, Pallas kernels, on_device(): pl.pallas_call(kernel, out_shape=jax.ShapeDtypeStruct(flat.shape, jnp.flo...  63.5 us

profile of v5, /device:TPU:25, one launch (start us, length us, event | category | flops | bytes accessed | tf_op | source)
XLA Modules:
  0.0 64.2 jit_solution(13410454761396463544)
XLA Ops:
  0.0 63.5 %shard_map.55 = f32[432,128]{1,0:T(8,128)S(1)} custom-call(f32[432,128]{1,0:T(8,128)} %bitcast.11, f32[96,96]{1,0:T(8,128)} %constant.8.clone.dealt_in, f32[96,96]{1,0:T(8,128)} %constant.9.clone.dealt_t_in, f32[256,256]{1,0:T(8,128)} %constant.10.clone.to_spectrum_in, f32[256,256]{1,0:T(8,128)} %constant.11.clone.from_spectrum_in), custom_call_target="tpu_custom_call" | custom-call | tf_op jit(solution)/shard_map/pallas_call | solution.py:346
  63.5 0.7 %copy.9 = f32[2,3,9216]{2,0,1:T(2,128)} copy(f32[2,3,9216]{2,0,1:T(2,128)S(1)} %bitcast.10) | data formatting | bytes 442368

commit v6 on v5

--- a/solution.py
+++ b/solution.py
@@ -286,6 +286,7 @@
     gather(*back_rest)
     for j in range(2):
         gather(*back_jobs[j])
+        planes = []
         for x in range(PLANES):
             plane = pl.ds(x * NG, NG)
             main = jnp.concatenate([get(returned.at[j], x * 4 + r) for r in range(PLANES)], axis=0)
@@ -298,16 +299,19 @@
                 table_times(dealt_t, jnp.concatenate([main, rest], axis=1)), from_spectrum
             )
             parts = [potential[:, :LANES], potential[:, LANES:]]
+            planes.append(parts)
             term = -(parts[0] * own[0, plane] + parts[1] * own[1, plane])
             for k, value in enumerate(packed_rows(term)):
                 terms[j, pl.ds(x * TILES + k, TURNS, stride=3), :] = value
+        term_swaps[j].start()
+        for x in range(PLANES):
+            plane = pl.ds(x * NG, NG)
             for i in range(2):
-                mine = parts[i] * partner[j, plane]
+                mine = planes[x][i] * partner[j, plane]
                 if j == 0:
                     to_own[i, plane] = -mine
                 else:
                     to_own[i, plane] = to_own[i, plane] - mine
-        term_swaps[j].start()
         if j == 0:
             drain(*back_jobs[0])
             drain(*back_rest)

time: 64.8 us -> 64.8 us (level)
  no operation moved by 1% of the time
where the time goes in v6:
time: 64.8 us; the launch traced here: 64.2 us
  Pallas kernels  63.5 us (98%)
  local copies, waits for them, and re-layouts  0.69 us (1%)
    pallas_call x1, Pallas kernels, on_device(): pl.pallas_call(kernel, out_shape=jax.ShapeDtypeStruct(flat.shape, jnp.flo...  63.5 us

profile of v6, /device:TPU:25, one launch (start us, length us, event | category | flops | bytes accessed | tf_op | source)
XLA Modules:
  0.0 64.2 jit_solution(16957070950824082261)
XLA Ops:
  0.0 63.5 %shard_map.55 = f32[432,128]{1,0:T(8,128)S(1)} custom-call(f32[432,128]{1,0:T(8,128)} %bitcast.11, f32[96,96]{1,0:T(8,128)} %constant.8.clone.dealt_in, f32[96,96]{1,0:T(8,128)} %constant.9.clone.dealt_t_in, f32[256,256]{1,0:T(8,128)} %constant.10.clone.to_spectrum_in, f32[256,256]{1,0:T(8,128)} %constant.11.clone.from_spectrum_in), custom_call_target="tpu_custom_call" | custom-call | tf_op jit(solution)/shard_map/pallas_call | solution.py:350
  63.5 0.7 %copy.9 = f32[2,3,9216]{2,0,1:T(2,128)} copy(f32[2,3,9216]{2,0,1:T(2,128)S(1)} %bitcast.10) | data formatting | bytes 442368

commit v7 on v6

--- a/solution.py
+++ b/solution.py
@@ -286,18 +286,22 @@
     gather(*back_rest)
     for j in range(2):
         gather(*back_jobs[j])
-        planes = []
-        for x in range(PLANES):
-            plane = pl.ds(x * NG, NG)
-            main = jnp.concatenate([get(returned.at[j], x * 4 + r) for r in range(PLANES)], axis=0)
+        columns = []
+        for x in range(PLANES):
+            main = [get(returned.at[j], x * 4 + r) for r in range(PLANES)]
+            columns.append(jnp.concatenate(main, axis=0))
             both = get(returned.at[j], x * 4 + 3)
             last = get(returned_rest, x)
             if j == 1:
                 last = turned(last)
-            rest = jnp.concatenate([both, turned(both), last], axis=0)
-            potential = times_table(
-                table_times(dealt_t, jnp.concatenate([main, rest], axis=1)), from_spectrum
-            )
+            columns.append(jnp.concatenate([both, turned(both), last], axis=0))
+        side_by_side = table_times(dealt_t, jnp.concatenate(columns, axis=1))
+        spectra = [side_by_side[:, 2 * x * LANES : 2 * (x + 1) * LANES] for x in range(PLANES)]
+        potentials = times_table(jnp.concatenate(spectra, axis=0), from_spectrum)
+        planes = []
+        for x in range(PLANES):
+            plane = pl.ds(x * NG, NG)
+            potential = potentials[x * NG : (x + 1) * NG]
             parts = [potential[:, :LANES], potential[:, LANES:]]
             planes.append(parts)
             term = -(parts[0] * own[0, plane] + parts[1] * own[1, plane])

time: 64.8 us -> 64.9 us (level)
  no operation moved by 1% of the time
where the time goes in v7:
time: 64.9 us; the launch traced here: 64.2 us
  Pallas kernels  63.5 us (98%)
  local copies, waits for them, and re-layouts  0.69 us (1%)
    pallas_call x1, Pallas kernels, on_device(): pl.pallas_call(kernel, out_shape=jax.ShapeDtypeStruct(flat.shape, jnp.flo...  63.5 us

profile of v7, /device:TPU:25, one launch (start us, length us, event | category | flops | bytes accessed | tf_op | source)
XLA Modules:
  0.0 64.2 jit_solution(16879425280461302940)
XLA Ops:
  0.0 63.5 %shard_map.55 = f32[432,128]{1,0:T(8,128)S(1)} custom-call(f32[432,128]{1,0:T(8,128)} %bitcast.11, f32[96,96]{1,0:T(8,128)} %constant.8.clone.dealt_in, f32[96,96]{1,0:T(8,128)} %constant.9.clone.dealt_t_in, f32[256,256]{1,0:T(8,128)} %constant.10.clone.to_spectrum_in, f32[256,256]{1,0:T(8,128)} %constant.11.clone.from_spectrum_in), custom_call_target="tpu_custom_call" | custom-call | tf_op jit(solution)/shard_map/pallas_call | solution.py:354
  63.5 0.7 %copy.9 = f32[2,3,9216]{2,0,1:T(2,128)} copy(f32[2,3,9216]{2,0,1:T(2,128)S(1)} %bitcast.10) | data formatting | bytes 442368
